TPU v7x, 32 devices: a whole 2x2x4 slice. The times are simulated.
32 devices in a mesh: panel: 2 (over core), colat: 4 (over z), lon: 4 (over y, x).
Axes of the slice: x: 2, y: 2, z: 4, core: 2. Of those that a mesh axis runs over, the one named last changes fastest.
Arguments:
- state: float32 [2, 4, 8, 128, 512], P('panel', None, None, 'lon', 'colat'), may hold values from -6 to 6
- rhs: float32 [2, 4, 8, 128, 512], P('panel', None, None, 'lon', 'colat'), may hold values from -6 to 6
- viscosity: float32 [2, 8, 128, 512], P('panel', None, 'lon', 'colat'), may hold values from 0.25 to 4
- radial_bounds: int32 [2, 2], P('panel'), may hold values from 0 to 8, as said below
- partner_device: int32 [2, 4, 4, 8], P('panel', 'colat', 'lon'), may hold values from 0 to 15, as said below
- ghost_source: int32 [2, 4, 4, 8, 20], P('panel', 'colat', 'lon'), may hold values from 0 to 3966, as said below
- ghost_target: int32 [2, 4, 4, 8, 20], P('panel', 'colat', 'lon'), may hold values from 0 to 320, as said below
- interp_weights: float32 [2, 4, 4, 8, 4, 20], P('panel', 'colat', 'lon'), may hold values from 0 to 1, as said below
- rotation: float32 [2, 4, 4, 8, 20], P('panel', 'colat', 'lon'), may hold values from -3.140625 to 3.140625
Outputs:
- state_out: float32 [2, 4, 8, 128, 512], P('panel', None, None, 'lon', 'colat')
- residual: float32 [2, 4, 8, 128, 512], P('panel', None, None, 'lon', 'colat')
Inputs may be any that keep to these rules, and one draw needn't show every extreme that they name: For each panel a, radial_bounds[a, 0] < 4 and radial_bounds[a, 1] > 4. `partner_device`: A device's 8 partners are distinct devices of the other panel, numbered colatitude block times 4 plus longitude block; they are consecutive numbers counted round and include the number one below the device's own number. `ghost_source`: A value p * 128 + t with t < 127 and p < 31, local to the partner's block. `ghost_target`: each ghost cell of a device that lies beyond an edge of the panel is named by exactly one of that device's slots and no other ghost cell by any; used slots come first in the order partner, slot, and unused ones hold 320. `interp_weights`: the four weights of a slot are nonnegative and sum to one.
All inputs are finite; a program needn't handle non-finite values.
Results may differ from a plain program's by a relative error of at most 0.0003.
Values sent between devices are 32-bit elements; how exact they have to be, the bound alone decides.
A program may use at most 128 MiB of HBM per device.

v0:
```python
import jax
import jax.numpy as jnp
from jax import lax
from jax.experimental import pallas as pl
from jax.experimental.pallas import tpu as pltpu
from jax.sharding import PartitionSpec as P

OMEGA = 0.6
PRESSURE_STEP = 0.25
PEERS = 15
F32 = jnp.float32
BF16 = jnp.bfloat16
MESH = pl.DeviceIdType.MESH


def kernel(colats, lons, act_ref, state_ref, rhs_ref, visc_ref, req_ref, cs_ref,
           xo_ref, ro_ref,
           mk, ve, klon, kcu, kcd, kru, krd, dg, dinv, whi, wlo, oh, rx,
           slon, rlon, scol, rcol, vscol, vrcol, vrlon, sg, rg,
           hsend, hrecv, gsend, grecv):
    width = state_ref.shape[1]
    count = colats * lons
    panel = lax.axis_index("panel")
    colat = lax.axis_index("colat")
    lon = lax.axis_index("lon")
    me = colat * lons + lon

    def other(offset):
        number = lax.rem(me + offset + count, count)
        return (1 - panel, lax.div(number, lons), lax.rem(number, lons))

    lon_dn = (panel, colat, lax.rem(lon + lons - 1, lons))
    lon_up = (panel, colat, lax.rem(lon + 1, lons))
    col_dn = (panel, lax.rem(colat + colats - 1, colats), lon)
    col_up = (panel, lax.rem(colat + 1, colats), lon)

    barrier = pltpu.get_barrier_semaphore()
    greeted = [o for o in range(-8, 9)][: min(17, count)]
    for offset in greeted:
        pl.semaphore_signal(barrier, inc=1, device_id=other(offset), device_id_type=MESH)
    for target in (lon_dn, lon_up, col_dn, col_up):
        pl.semaphore_signal(barrier, inc=1, device_id=target, device_id_type=MESH)

    lane = lax.broadcasted_iota(jnp.int32, (8, 128), 1)
    row = lax.broadcasted_iota(jnp.int32, (8, 128), 0)
    first_lane = lane == 0
    last_lane = lane == 127
    top = row == 7
    bottom = row == 0
    act = act_ref[...]
    has_lon_dn = jnp.where(lon > 0, 1.0, 0.0).astype(F32)
    has_lon_up = jnp.where(lon < lons - 1, 1.0, 0.0).astype(F32)
    has_col_dn = jnp.where(colat > 0, 1.0, 0.0).astype(F32)
    has_col_up = jnp.where(colat < colats - 1, 1.0, 0.0).astype(F32)
    zero = jnp.zeros((8, 128), F32)

    def rad_up(x):
        return jnp.where(top, 0.0, pltpu.roll(x, 7, 0))

    def rad_dn(x):
        return jnp.where(bottom, 0.0, pltpu.roll(x, 1, 0))

    def cup(x, halo, i):
        return jnp.where(last_lane, pltpu.roll(halo, 127 - i, 1), pltpu.roll(x, 127, 1))

    def cdn(x, halo, i):
        return jnp.where(first_lane, pltpu.roll(halo, lax.rem(128 - i, 128), 1), pltpu.roll(x, 1, 1))

    def pack(x, i, low, high):
        here = lane == i
        low = jnp.where(here, pltpu.roll(x, i, 1), low)
        high = jnp.where(here, pltpu.roll(x, lax.rem(i + 1, 128), 1), high)
        return low, high

    def send(src, dst, k, target, sends, recvs):
        return pltpu.make_async_remote_copy(
            src_ref=src, dst_ref=dst, send_sem=sends.at[k], recv_sem=recvs.at[k],
            device_id=target, device_id_type=MESH)

    def first(p, carry):
        low, high, vlow, vhigh = carry
        for c in range(4):
            x = state_ref[c, p] * act
            mk[0, c, p + 1] = x
            low, high = pack(x, c * 32 + p, low, high)
        e = visc_ref[p]
        ve[p + 1] = e
        vlow, vhigh = pack(e, p, vlow, vhigh)
        return low, high, vlow, vhigh

    low, high, vlow, vhigh = lax.fori_loop(0, width, first, (zero, zero, zero, zero))
    vscol[0] = vlow
    vscol[1] = vhigh
    rx[15] = zero
    for r in range(3):
        rg[r, 15] = zero

    pl.semaphore_wait(barrier, len(greeted) + 4)

    def request(m):
        return send(req_ref.at[m], rx.at[m], 45 + m, other(m - 8), gsend, grecv)

    def start_request(m, _):
        request(m).start()
        return 0

    lax.fori_loop(0, PEERS, start_request, 0)

    def halo_copies(r):
        return [
            send(slon.at[r, 0], rlon.at[r, 1], 4 * r + 0, lon_dn, hsend, hrecv),
            send(slon.at[r, 1], rlon.at[r, 0], 4 * r + 1, lon_up, hsend, hrecv),
            send(scol.at[r, 0], rcol.at[r, 1], 4 * r + 2, col_dn, hsend, hrecv),
            send(scol.at[r, 1], rcol.at[r, 0], 4 * r + 3, col_up, hsend, hrecv),
        ]

    visc_copies = [
        send(visc_ref.at[0], vrlon.at[1], 12, lon_dn, hsend, hrecv),
        send(visc_ref.at[width - 1], vrlon.at[0], 13, lon_up, hsend, hrecv),
        send(vscol.at[0], vrcol.at[1], 14, col_dn, hsend, hrecv),
        send(vscol.at[1], vrcol.at[0], 15, col_up, hsend, hrecv),
    ]
    for copy in visc_copies:
        copy.start()

    def start_halos(r, low, high):
        for c in range(4):
            slon[r, 0, c] = mk[r % 2, c, 1]
            slon[r, 1, c] = mk[r % 2, c, width]
        scol[r, 0] = low
        scol[r, 1] = high
        for copy in halo_copies(r):
            copy.start()

    start_halos(0, low, high)

    req = req_ref[...].reshape(128, 128)
    column = lax.broadcasted_iota(jnp.int32, (128, 384), 1)
    for j in range(3):
        goal = req[:, 15 + j : 16 + j].astype(jnp.int32) + 320
        oh[j * 128 : (j + 1) * 128, :] = jnp.where(column == goal, 1.0, 0.0).astype(BF16)

    def wait_request(m, _):
        request(m).wait_recv()
        return 0

    lax.fori_loop(0, PEERS, wait_request, 0)
    asked = rx[...].reshape(128, 128)
    wide = lax.broadcasted_iota(jnp.int32, (128, 128), 1)
    for j in range(3):
        src = asked[:, 5 * j : 5 * j + 1].astype(jnp.int32)
        w = [asked[:, 5 * j + 1 + k : 5 * j + 2 + k] for k in range(4)]
        src = jnp.broadcast_to(src, (128, 128))
        src_p = lax.shift_right_logical(src, 7)
        src_t = src - src_p * 128
        near = wide == src_t
        far = wide == src_t + 1
        parts = []
        for a, b in ((w[0], w[1]), (w[2], w[3])):
            u = jnp.where(near, a, jnp.where(far, b, 0.0))
            hi = u.astype(BF16).astype(F32)
            parts.append((hi, u - hi))
        rows = pl.ds(j * 128, 128)

        def build(pp, _, src_p=src_p, parts=parts, rows=rows):
            for h in range(2):
                p = 2 * pp + h
                here = src_p == p
                above = src_p == p - 1
                cols = pl.ds(h * 128, 128)
                whi[pp, rows, cols] = jnp.where(here, parts[0][0], jnp.where(above, parts[1][0], 0.0)).astype(BF16)
                wlo[pp, rows, cols] = jnp.where(here, parts[0][1], jnp.where(above, parts[1][1], 0.0)).astype(BF16)
            return 0

        lax.fori_loop(0, width // 2, build, 0)

    def answer(r, m):
        return send(sg.at[r, m], rg.at[r, m], 15 * r + m, other(8 - m), gsend, grecv)

    nt = (((1,), (1,)), ((), ()))

    def start_answers(r):
        def step(pp, acc):
            x = jnp.concatenate(
                [mk[r % 2, :, 2 * pp + 1].reshape(32, 128), mk[r % 2, :, 2 * pp + 2].reshape(32, 128)], axis=1)
            hi = x.astype(BF16)
            lo = (x - hi.astype(F32)).astype(BF16)
            a = whi[pp]
            acc = acc + lax.dot_general(a, hi, nt, preferred_element_type=F32)
            acc = acc + lax.dot_general(a, lo, nt, preferred_element_type=F32)
            return acc + lax.dot_general(wlo[pp], hi, nt, preferred_element_type=F32)

        v = lax.fori_loop(0, width // 2, step, jnp.zeros((384, 32), F32))
        packed = jnp.concatenate([v[:128], v[128:256], v[256:], jnp.zeros((128, 32), F32)], axis=1)
        sg[r] = packed.reshape(16, 8, 128)

        def go(m, _):
            answer(r, m).start()
            return 0

        lax.fori_loop(0, PEERS, go, 0)

    start_answers(0)

    for copy in visc_copies:
        copy.wait_recv()
    ve[0] = vrlon[0] * has_lon_dn
    ve[width + 1] = vrlon[1] * has_lon_up
    vlow = vrcol[0] * has_col_dn
    vhigh = vrcol[1] * has_col_up
    klon[0] = 0.5 * (ve[0] + ve[1])

    def links(p, _):
        e = ve[p + 1]
        ru = 0.5 * (e + rad_up(e))
        rd = 0.5 * (e + rad_dn(e))
        lu = 0.5 * (e + ve[p + 2])
        ld = 0.5 * (e + ve[p])
        cu = 0.5 * (e + cup(e, vhigh, p))
        cd = 0.5 * (e + cdn(e, vlow, p))
        d = ru + rd + lu + ld + cu + cd
        klon[p + 1] = lu
        kcu[p] = cu
        kcd[p] = cd
        kru[p] = ru
        krd[p] = rd
        dg[p] = d
        dinv[p] = OMEGA / d
        return 0

    lax.fori_loop(0, width, links, 0)

    for r in range(3):
        now, later = r % 2, (r + 1) % 2
        if r > 0:
            start_halos(r, low, high)
            start_answers(r)
        for copy in halo_copies(r):
            copy.wait_recv()

        def wait_answer(m, _, r=r):
            answer(r, m).wait_recv()
            return 0

        lax.fori_loop(0, PEERS, wait_answer, 0)
        turned = jnp.transpose(rg[r].reshape(128, 128))
        vals = jnp.concatenate([turned[0:32], turned[32:64], turned[64:96]], axis=1)
        a = vals.astype(BF16)
        rest = vals - a.astype(F32)
        b = rest.astype(BF16)
        d = (rest - b.astype(F32)).astype(BF16)
        spread = jnp.dot(jnp.concatenate([a, b, d], axis=0), oh[...], preferred_element_type=F32)
        ghost = spread[0:32] + spread[32:64] + spread[64:96]
        cosine = cs_ref[0:1, :]
        sine = cs_ref[1:2, :]
        parts = [ghost[0:8], cosine * ghost[8:16] - sine * ghost[16:24],
                 sine * ghost[8:16] + cosine * ghost[16:24], ghost[24:32]]
        halo_lo = rcol[r, 0] * has_col_dn
        halo_hi = rcol[r, 1] * has_col_up
        for c in range(4):
            mk[now, c, 0] = rlon[r, 0, c] * has_lon_dn + parts[c][:, 0:128]
            mk[now, c, width + 1] = rlon[r, 1, c] * has_lon_up + parts[c][:, 128:256]
            tail = parts[c][:, 256:384]
            inside = (lane >= 32 * c) & (lane < 32 * c + 32)
            lo_part = pltpu.roll(tail, 32 * c, 1) if c else tail
            hi_part = pltpu.roll(tail, (32 * c + 96) % 128, 1) if c != 1 else tail
            halo_lo = halo_lo + jnp.where(inside, lo_part, 0.0)
            halo_hi = halo_hi + jnp.where(inside, hi_part, 0.0)
        source = state_ref if r == 0 else xo_ref

        def sweep(p, carry, r=r, now=now, later=later, halo_lo=halo_lo, halo_hi=halo_hi, source=source):
            low, high = carry
            ru, rd = kru[p], krd[p]
            lu, ld = klon[p + 1], klon[p]
            cu, cd = kcu[p], kcd[p]
            d = dg[p]
            pressure = mk[now, 3, p + 1]
            grad = (pressure - rad_dn(pressure), pressure - cdn(pressure, halo_lo, 96 + p),
                    pressure - mk[now, 3, p])
            div = zero
            res = []
            for c in range(3):
                x = mk[now, c, p + 1]
                i = c * 32 + p
                xru, xlu, xcu = rad_up(x), mk[now, c, p + 2], cup(x, halo_hi, i)
                around = ru * xru + rd * rad_dn(x) + lu * xlu + ld * mk[now, c, p]
                around = around + cu * xcu + cd * cdn(x, halo_lo, i)
                div = div + ((xru, xcu, xlu)[c] - x)
                res.append(act * (rhs_ref[c, p] - ((d * x - around) + grad[c])))
            res.append(act * (rhs_ref[3, p] + div))
            if r == 2:
                for c in range(4):
                    ro_ref[c, p] = res[c]
                return carry
            scale = dinv[p]
            for c in range(4):
                step = scale * res[c] if c < 3 else -PRESSURE_STEP * ve[p + 1] * res[c]
                x = source[c, p] + step
                xo_ref[c, p] = x
                x = x * act
                mk[later, c, p + 1] = x
                low, high = pack(x, c * 32 + p, low, high)
            return low, high

        low, high = lax.fori_loop(0, width, sweep, (zero, zero))

    for copy in visc_copies:
        copy.wait_send()
    for r in range(3):
        for copy in halo_copies(r):
            copy.wait_send()

    def drain(m, _):
        request(m).wait_send()
        for r in range(3):
            answer(r, m).wait_send()
        return 0

    lax.fori_loop(0, PEERS, drain, 0)


def per_device(state, rhs, viscosity, radial_bounds, partner_device, ghost_source,
               ghost_target, interp_weights, rotation):
    components, levels, width_p, width_t = state.shape[1:]
    colats, lons = lax.axis_size("colat"), lax.axis_size("lon")
    count = colats * lons
    me = lax.axis_index("colat") * lons + lax.axis_index("lon")
    level_ids = jnp.arange(levels)
    active = ((level_ids >= radial_bounds[0, 0]) & (level_ids < radial_bounds[0, 1])).astype(F32)
    act = jnp.broadcast_to(active[:, None], (levels, width_t))
    partners = partner_device[0, 0, 0]
    targets = ghost_target[0, 0, 0]
    fields = jnp.concatenate(
        [ghost_source[0, 0, 0].astype(F32)[:, None], interp_weights[0, 0, 0],
         (targets - 320).astype(F32)[:, None]], axis=1)
    fields = jnp.pad(fields, ((0, 0), (0, 0), (0, 4))).reshape(8, 6, 3, 8)
    asks = jnp.transpose(fields[:, :5], (0, 3, 2, 1)).reshape(8, 8, 15)
    goals = jnp.transpose(fields[:, 5], (0, 2, 1))
    rows = jnp.pad(jnp.concatenate([asks, goals], axis=2), ((0, 0), (0, 0), (0, 110)))
    peer = jnp.mod(partners - me + 8 + count, count)
    match = jnp.arange(16)[:, None] == peer[None, :]
    req = jnp.sum(jnp.where(match[:, :, None, None], rows[None], 0.0), axis=1)
    named = targets.reshape(-1)[:, None] == jnp.arange(384)[None, :]
    named = named & (jnp.arange(384)[None, :] < 320)
    angle = jnp.sum(jnp.where(named, rotation[0, 0, 0].reshape(-1)[:, None], 0.0), axis=0)
    cs = jnp.stack([jnp.cos(angle), jnp.sin(angle)])
    block = (components, width_p, levels, width_t)
    vm = pltpu.VMEM
    tile = (levels, width_t)
    row_tiles = (width_p,) + tile
    xo, ro = pl.pallas_call(
        lambda *refs: kernel(colats, lons, *refs),
        out_shape=[jax.ShapeDtypeStruct(block, F32)] * 2,
        in_specs=[pl.BlockSpec(memory_space=pltpu.VMEM)] * 6,
        out_specs=[pl.BlockSpec(memory_space=pltpu.VMEM)] * 2,
        scratch_shapes=[
            vm((2, components, width_p + 2) + tile, F32),
            vm((width_p + 2,) + tile, F32),
            vm((width_p + 1,) + tile, F32),
            vm(row_tiles, F32), vm(row_tiles, F32), vm(row_tiles, F32), vm(row_tiles, F32),
            vm(row_tiles, F32), vm(row_tiles, F32),
            vm((width_p // 2, 384, 256), BF16), vm((width_p // 2, 384, 256), BF16),
            vm((384, 384), BF16),
            vm((16,) + tile, F32),
            vm((3, 2, components) + tile, F32), vm((3, 2, components) + tile, F32),
            vm((3, 2) + tile, F32), vm((3, 2) + tile, F32),
            vm((2,) + tile, F32), vm((2,) + tile, F32), vm((2,) + tile, F32),
            vm((3, 16) + tile, F32), vm((3, 16) + tile, F32),
            pltpu.SemaphoreType.DMA((16,)), pltpu.SemaphoreType.DMA((16,)),
            pltpu.SemaphoreType.DMA((60,)), pltpu.SemaphoreType.DMA((60,)),
        ],
        compiler_params=pltpu.CompilerParams(
            collective_id=0, has_side_effects=True, vmem_limit_bytes=32 * 1024 * 1024),
        name="sweeps",
    )(act, jnp.transpose(state[0], (0, 2, 1, 3)), jnp.transpose(rhs[0], (0, 2, 1, 3)),
      jnp.transpose(viscosity[0], (1, 0, 2)), req, cs)
    back = lambda x: jnp.transpose(x, (0, 2, 1, 3))[None]
    return back(xo), back(ro)


def solution(mesh):
    field = P("panel", None, None, "lon", "colat")
    return jax.shard_map(
        per_device,
        mesh=mesh,
        in_specs=(
            field,
            field,
            P("panel", None, "lon", "colat"),
            P("panel", None),
            P("panel", "colat", "lon", None),
            P("panel", "colat", "lon", None, None),
            P("panel", "colat", "lon", None, None),
            P("panel", "colat", "lon", None, None, None),
            P("panel", "colat", "lon", None, None),
        ),
        out_specs=(field, field),
        check_vma=False,
    )
```

profile of v0, /device:TPU:0, one launch (start us, length us, event | category | flops | bytes accessed | tf_op | source)
XLA Modules:
  0.0 66.1 jit_solution(15043763435188441543)
XLA Ops:
  0.6 0.0 copy-start.8
  0.6 0.0 copy-start.5
  0.7 0.6 copy-done.8
  1.3 0.0 copy-start.4
  1.3 0.0 copy-done.5
  1.3 0.1 broadcast_in_dim.58
  1.4 0.6 copy-done.4
  2.0 0.1 eq.37
  2.1 0.0 copy-start.7
  2.1 0.1 select_reduce_fusion.1
  2.2 0.5 copy-done.7
  2.7 0.6 fusion.3
  3.3 1.3 %and_convert_fusion = f32[8]{0:T(128)S(1)} fusion(s32[]{:T(128)} %bitcast.1, s32[]{:T(128)} %bitcast), kind=kLoop, calls=%fused_computation.19 | loop fusion | flops 32 | bytes 40 | tf_op jit(solution)/shard_map/convert_element_type | solution.py:329
  4.7 0.0 copy-start.6
  4.7 0.0 copy-start.3
  4.7 0.1 broadcast_in_dim.54.refs_0_
  4.8 0.6 copy-done.6
  5.4 0.0 copy-done.3
  5.4 0.0 copy-start.2
  5.5 0.0 copy-start
  5.5 0.0 copy-start.1
  5.5 0.1 reshape.109
  5.6 0.1 copy.40
  5.8 0.1 copy.41
  5.9 0.1 select_maximum_fusion
  6.0 0.2 select_reduce_fusion.refs_4_
  6.2 0.1 copy-done.2
  6.3 0.1 copy.48
  6.4 0.1 copy-done
  6.5 0.2 copy-done.1
  6.7 0.6 copy_bitcast_fusion
  7.3 57.1 %sweeps.1 = (f32[4,32,8,128]{3,2,1,0:T(8,128)S(1)}, f32[4,32,8,128]{3,2,1,0:T(8,128)S(1)}) custom-call(f32[8,128]{1,0:T(8,128)S(1)} %broadcast_in_dim.54.refs_0_, f32[4,32,8,128]{3,2,1,0:T(8,128)S(1)} %get-tuple-element.19.refs_1_, f32[4,32,8,128]{3,2,1,0:T(8,128)S(1)} %get-tuple-element.18.refs_2_, f32[32,8,128]{2,1,0:T(8,128)S(1)} %bitcast.41, ...), custom_call_target="tpu_custom_call" | custom-call | tf_op jit(solution)/shard_map/sweeps/pallas_call | solution.py:351
  64.4 0.9 %copy.42 = f32[1,4,8,32,128]{4,3,2,1,0:T(8,128)} copy(f32[1,4,8,32,128]{4,2,3,1,0:T(8,128)S(1)} %bitcast.40) | data formatting | bytes 1048576
  65.3 0.9 %copy.43 = f32[1,4,8,32,128]{4,3,2,1,0:T(8,128)} copy(f32[1,4,8,32,128]{4,2,3,1,0:T(8,128)S(1)} %bitcast.39) | data formatting | bytes 1048576
  (15 shorter events, 0.1 us)
Async XLA Ops:
  0.6 0.7 copy-start.8
  0.6 0.7 %copy-start.5 = (f32[1,1,1,8,20]{4,3,2,1,0:T(8,128)S(1)}, f32[1,1,1,8,20]{4,3,2,1,0:T(8,128)}, u32[]{:S(2)}) copy-start(f32[1,1,1,8,20]{4,3,2,1,0:T(8,128)} %param.17) | copy-start | bytes 1924
  1.3 0.7 %copy-start.4 = (s32[1,1,1,8,20]{4,3,2,1,0:T(8,128)S(1)}, s32[1,1,1,8,20]{4,3,2,1,0:T(8,128)}, u32[]{:S(2)}) copy-start(s32[1,1,1,8,20]{4,3,2,1,0:T(8,128)} %param.15) | copy-start | bytes 1924
  2.1 0.7 copy-start.7
  4.7 0.7 %copy-start.6 = (s32[1,1,1,8,20]{4,3,2,1,0:T(8,128)S(1)}, s32[1,1,1,8,20]{4,3,2,1,0:T(8,128)}, u32[]{:S(2)}) copy-start(s32[1,1,1,8,20]{4,3,2,1,0:T(8,128)} %param.14) | copy-start | bytes 1924
  4.7 0.7 %copy-start.3 = (f32[1,1,1,8,4,20]{5,4,3,2,1,0:T(4,128)S(1)}, f32[1,1,1,8,4,20]{5,4,3,2,1,0:T(4,128)}, u32[]{:S(2)}) copy-start(f32[1,1,1,8,4,20]{5,4,3,2,1,0:T(4,128)} %param.16) | copy-start | bytes 7684
  5.4 0.9 %copy-start.2 = (f32[1,8,32,128]{3,2,1,0:T(8,128)S(1)}, f32[1,8,32,128]{3,2,1,0:T(8,128)}, u32[]{:S(2)}) copy-start(f32[1,8,32,128]{3,2,1,0:T(8,128)} %param.11) | copy-start | bytes 393220
  5.5 1.1 %copy-start = (f32[1,4,8,32,128]{4,3,2,1,0:T(8,128)S(1)}, f32[1,4,8,32,128]{4,3,2,1,0:T(8,128)}, u32[]{:S(2)}) copy-start(f32[1,4,8,32,128]{4,3,2,1,0:T(8,128)} %param.10) | copy-start | bytes 1572868
  5.5 1.2 %copy-start.1 = (f32[1,4,8,32,128]{4,3,2,1,0:T(8,128)S(1)}, f32[1,4,8,32,128]{4,3,2,1,0:T(8,128)}, u32[]{:S(2)}) copy-start(f32[1,4,8,32,128]{4,3,2,1,0:T(8,128)} %param.9) | copy-start | bytes 1572868
where the time goes:
time: 66.5 us; the launch traced here: 66.1 us
  Pallas kernels  57.1 us (86%)
  local copies, waits for them, and re-layouts  6.51 us (10%)
  other arithmetic  1.77 us (3%)
  between operations  0.81 us (1%)
    pallas_call x1, Pallas kernels, per_device(): pl.pallas_call(lambda *refs: kernel(colats, lons, *refs), out_shape=[jax....  57.1 us
    unnamed x22, local copies, waits for them, and re-layouts  4.67 us

commit v1 on v0

--- a/solution.py
+++ b/solution.py
@@ -13,9 +13,18 @@
 MESH = pl.DeviceIdType.MESH
 
 
-def kernel(colats, lons, act_ref, state_ref, rhs_ref, visc_ref, req_ref, cs_ref,
+def blocked(steps, unroll, body, init):
+    def block(q, carry):
+        for h in range(unroll):
+            carry = body(q * unroll + h, carry)
+        return carry
+
+    return lax.fori_loop(0, steps // unroll, block, init)
+
+
+def kernel(colats, lons, bounds_ref, partner_ref, state_ref, rhs_ref, visc_ref, src_ref, tgt_ref, w_ref, rot_ref,
            xo_ref, ro_ref,
-           mk, ve, klon, kcu, kcd, kru, krd, dg, dinv, whi, wlo, oh, rx,
+           mk, ve, klon, kcu, kcd, kru, krd, dg, dinv, whi, wlo, mhl, oh, fx, req_ref, rx,
            slon, rlon, scol, rcol, vscol, vrcol, vrlon, sg, rg,
            hsend, hrecv, gsend, grecv):
     width = state_ref.shape[1]
@@ -47,7 +56,7 @@
     last_lane = lane == 127
     top = row == 7
     bottom = row == 0
-    act = act_ref[...]
+    act = jnp.where((row >= bounds_ref[0, 0]) & (row < bounds_ref[0, 1]), 1.0, 0.0).astype(F32)
     has_lon_dn = jnp.where(lon > 0, 1.0, 0.0).astype(F32)
     has_lon_up = jnp.where(lon < lons - 1, 1.0, 0.0).astype(F32)
     has_col_dn = jnp.where(colat > 0, 1.0, 0.0).astype(F32)
@@ -77,34 +86,68 @@
             src_ref=src, dst_ref=dst, send_sem=sends.at[k], recv_sem=recvs.at[k],
             device_id=target, device_id_type=MESH)
 
+    def split(p, xs):
+        cols = pl.ds(pl.multiple_of(p * 128, 128), 128)
+        for h in range(2):
+            x = jnp.concatenate(xs[2 * h : 2 * h + 2], axis=0)
+            hi = x.astype(BF16)
+            mhl[16 * h : 16 * h + 16, cols] = hi
+            mhl[16 * h + 32 : 16 * h + 48, cols] = (x - hi.astype(F32)).astype(BF16)
+
+    slots = src_ref.shape[-1]
+    fx[...] = jnp.zeros((128, 128), F32)
+    fx[0:8, 0:slots] = src_ref[...].astype(F32)
+    for k in range(4):
+        fx[8 + 8 * k : 16 + 8 * k, 0:slots] = w_ref[:, k, :]
+    fx[40:48, 0:slots] = (tgt_ref[...] - 320).astype(F32)
+    fx[48:56, 0:slots] = rot_ref[...]
+    by_slot = jnp.transpose(fx[...])
+    eighth = lane & 7
+    peer = jnp.zeros((8, 128), jnp.int32)
+    for k in range(8):
+        away = partner_ref[k] - me + 8
+        away = jnp.where(away < 0, away + count, away)
+        away = jnp.where(away >= count, away - count, away)
+        peer = jnp.where(eighth == k, away, peer)
+    for m in range(PEERS):
+        tile = zero
+        for j in range(3):
+            t = jnp.where(peer == m, by_slot[8 * j : 8 * j + 8], 0.0)
+            for shift in (127, 126, 124):
+                t = t + pltpu.roll(t, shift, 1)
+            tile = jnp.where(eighth == j, pltpu.roll(t, j, 1) if j else t, tile)
+        req_ref[m] = tile
+    req_ref[15] = zero
+    rx[15] = zero
+    for r in range(3):
+        rg[r, 15] = zero
+
+    pl.semaphore_wait(barrier, len(greeted) + 4)
+
+    def request(m):
+        return send(req_ref.at[m], rx.at[m], 3, other(m - 8), gsend, grecv)
+
+    for m in range(PEERS):
+        request(m).start()
+
+    everything = pl.ds(0, PEERS)
+    requests = send(req_ref.at[everything], rx.at[everything], 3, other(-8), gsend, grecv)
+
     def first(p, carry):
         low, high, vlow, vhigh = carry
-        for c in range(4):
-            x = state_ref[c, p] * act
+        xs = [state_ref[c, p] * act for c in range(4)]
+        for c, x in enumerate(xs):
             mk[0, c, p + 1] = x
             low, high = pack(x, c * 32 + p, low, high)
+        split(p, xs)
         e = visc_ref[p]
         ve[p + 1] = e
         vlow, vhigh = pack(e, p, vlow, vhigh)
         return low, high, vlow, vhigh
 
-    low, high, vlow, vhigh = lax.fori_loop(0, width, first, (zero, zero, zero, zero))
+    low, high, vlow, vhigh = blocked(width, 8, first, (zero, zero, zero, zero))
     vscol[0] = vlow
     vscol[1] = vhigh
-    rx[15] = zero
-    for r in range(3):
-        rg[r, 15] = zero
-
-    pl.semaphore_wait(barrier, len(greeted) + 4)
-
-    def request(m):
-        return send(req_ref.at[m], rx.at[m], 45 + m, other(m - 8), gsend, grecv)
-
-    def start_request(m, _):
-        request(m).start()
-        return 0
-
-    lax.fori_loop(0, PEERS, start_request, 0)
 
     def halo_copies(r):
         return [
@@ -136,20 +179,21 @@
 
     req = req_ref[...].reshape(128, 128)
     column = lax.broadcasted_iota(jnp.int32, (128, 384), 1)
+    angle = jnp.zeros((1, 384), F32)
     for j in range(3):
-        goal = req[:, 15 + j : 16 + j].astype(jnp.int32) + 320
-        oh[j * 128 : (j + 1) * 128, :] = jnp.where(column == goal, 1.0, 0.0).astype(BF16)
-
-    def wait_request(m, _):
-        request(m).wait_recv()
-        return 0
-
-    lax.fori_loop(0, PEERS, wait_request, 0)
+        goal = req[:, 40 + j : 41 + j].astype(jnp.int32) + 320
+        here = column == goal
+        oh[j * 128 : (j + 1) * 128, :] = jnp.where(here, 1.0, 0.0).astype(BF16)
+        angle = angle + jnp.sum(jnp.where(here, req[:, 48 + j : 49 + j], 0.0), axis=0, keepdims=True)
+    cosine = jnp.cos(angle)
+    sine = jnp.sin(angle)
+
+    requests.wait_recv()
     asked = rx[...].reshape(128, 128)
     wide = lax.broadcasted_iota(jnp.int32, (128, 128), 1)
     for j in range(3):
-        src = asked[:, 5 * j : 5 * j + 1].astype(jnp.int32)
-        w = [asked[:, 5 * j + 1 + k : 5 * j + 2 + k] for k in range(4)]
+        src = asked[:, j : j + 1].astype(jnp.int32)
+        w = [asked[:, 8 + 8 * k + j : 9 + 8 * k + j] for k in range(4)]
         src = jnp.broadcast_to(src, (128, 128))
         src_p = lax.shift_right_logical(src, 7)
         src_t = src - src_p * 128
@@ -162,43 +206,32 @@
             parts.append((hi, u - hi))
         rows = pl.ds(j * 128, 128)
 
-        def build(pp, _, src_p=src_p, parts=parts, rows=rows):
-            for h in range(2):
-                p = 2 * pp + h
-                here = src_p == p
-                above = src_p == p - 1
-                cols = pl.ds(h * 128, 128)
-                whi[pp, rows, cols] = jnp.where(here, parts[0][0], jnp.where(above, parts[1][0], 0.0)).astype(BF16)
-                wlo[pp, rows, cols] = jnp.where(here, parts[0][1], jnp.where(above, parts[1][1], 0.0)).astype(BF16)
+        def build(p, _, src_p=src_p, parts=parts, rows=rows):
+            here = src_p == p
+            above = src_p == p - 1
+            cols = pl.ds(pl.multiple_of(p * 128, 128), 128)
+            whi[rows, cols] = jnp.where(here, parts[0][0], jnp.where(above, parts[1][0], 0.0)).astype(BF16)
+            wlo[rows, cols] = jnp.where(here, parts[0][1], jnp.where(above, parts[1][1], 0.0)).astype(BF16)
             return 0
 
-        lax.fori_loop(0, width // 2, build, 0)
+        blocked(width, 4, build, 0)
 
     def answer(r, m):
-        return send(sg.at[r, m], rg.at[r, m], 15 * r + m, other(8 - m), gsend, grecv)
+        return send(sg.at[r, m], rg.at[r, m], r, other(8 - m), gsend, grecv)
+
+    def answers(r):
+        return send(sg.at[r, everything], rg.at[r, everything], r, other(8), gsend, grecv)
 
     nt = (((1,), (1,)), ((), ()))
 
     def start_answers(r):
-        def step(pp, acc):
-            x = jnp.concatenate(
-                [mk[r % 2, :, 2 * pp + 1].reshape(32, 128), mk[r % 2, :, 2 * pp + 2].reshape(32, 128)], axis=1)
-            hi = x.astype(BF16)
-            lo = (x - hi.astype(F32)).astype(BF16)
-            a = whi[pp]
-            acc = acc + lax.dot_general(a, hi, nt, preferred_element_type=F32)
-            acc = acc + lax.dot_general(a, lo, nt, preferred_element_type=F32)
-            return acc + lax.dot_general(wlo[pp], hi, nt, preferred_element_type=F32)
-
-        v = lax.fori_loop(0, width // 2, step, jnp.zeros((384, 32), F32))
+        v = lax.dot_general(whi[...], mhl[...], nt, preferred_element_type=F32)
+        v = v[:, :32] + v[:, 32:] + lax.dot_general(wlo[...], mhl[:32], nt, preferred_element_type=F32)
         packed = jnp.concatenate([v[:128], v[128:256], v[256:], jnp.zeros((128, 32), F32)], axis=1)
         sg[r] = packed.reshape(16, 8, 128)
 
-        def go(m, _):
+        for m in range(PEERS):
             answer(r, m).start()
-            return 0
-
-        lax.fori_loop(0, PEERS, go, 0)
 
     start_answers(0)
 
@@ -228,7 +261,7 @@
         dinv[p] = OMEGA / d
         return 0
 
-    lax.fori_loop(0, width, links, 0)
+    blocked(width, 4, links, 0)
 
     for r in range(3):
         now, later = r % 2, (r + 1) % 2
@@ -238,11 +271,7 @@
         for copy in halo_copies(r):
             copy.wait_recv()
 
-        def wait_answer(m, _, r=r):
-            answer(r, m).wait_recv()
-            return 0
-
-        lax.fori_loop(0, PEERS, wait_answer, 0)
+        answers(r).wait_recv()
         turned = jnp.transpose(rg[r].reshape(128, 128))
         vals = jnp.concatenate([turned[0:32], turned[32:64], turned[64:96]], axis=1)
         a = vals.astype(BF16)
@@ -251,8 +280,6 @@
         d = (rest - b.astype(F32)).astype(BF16)
         spread = jnp.dot(jnp.concatenate([a, b, d], axis=0), oh[...], preferred_element_type=F32)
         ghost = spread[0:32] + spread[32:64] + spread[64:96]
-        cosine = cs_ref[0:1, :]
-        sine = cs_ref[1:2, :]
         parts = [ghost[0:8], cosine * ghost[8:16] - sine * ghost[16:24],
                  sine * ghost[8:16] + cosine * ghost[16:24], ghost[24:32]]
         halo_lo = rcol[r, 0] * has_col_dn
@@ -293,16 +320,19 @@
                     ro_ref[c, p] = res[c]
                 return carry
             scale = dinv[p]
+            xs = []
             for c in range(4):
                 step = scale * res[c] if c < 3 else -PRESSURE_STEP * ve[p + 1] * res[c]
                 x = source[c, p] + step
                 xo_ref[c, p] = x
                 x = x * act
                 mk[later, c, p + 1] = x
+                xs.append(x)
                 low, high = pack(x, c * 32 + p, low, high)
+            split(p, xs)
             return low, high
 
-        low, high = lax.fori_loop(0, width, sweep, (zero, zero))
+        low, high = blocked(width, 8, sweep, (zero, zero))
 
     for copy in visc_copies:
         copy.wait_send()
@@ -310,40 +340,15 @@
         for copy in halo_copies(r):
             copy.wait_send()
 
-    def drain(m, _):
-        request(m).wait_send()
-        for r in range(3):
-            answer(r, m).wait_send()
-        return 0
-
-    lax.fori_loop(0, PEERS, drain, 0)
+    requests.wait_send()
+    for r in range(3):
+        answers(r).wait_send()
 
 
 def per_device(state, rhs, viscosity, radial_bounds, partner_device, ghost_source,
                ghost_target, interp_weights, rotation):
     components, levels, width_p, width_t = state.shape[1:]
     colats, lons = lax.axis_size("colat"), lax.axis_size("lon")
-    count = colats * lons
-    me = lax.axis_index("colat") * lons + lax.axis_index("lon")
-    level_ids = jnp.arange(levels)
-    active = ((level_ids >= radial_bounds[0, 0]) & (level_ids < radial_bounds[0, 1])).astype(F32)
-    act = jnp.broadcast_to(active[:, None], (levels, width_t))
-    partners = partner_device[0, 0, 0]
-    targets = ghost_target[0, 0, 0]
-    fields = jnp.concatenate(
-        [ghost_source[0, 0, 0].astype(F32)[:, None], interp_weights[0, 0, 0],
-         (targets - 320).astype(F32)[:, None]], axis=1)
-    fields = jnp.pad(fields, ((0, 0), (0, 0), (0, 4))).reshape(8, 6, 3, 8)
-    asks = jnp.transpose(fields[:, :5], (0, 3, 2, 1)).reshape(8, 8, 15)
-    goals = jnp.transpose(fields[:, 5], (0, 2, 1))
-    rows = jnp.pad(jnp.concatenate([asks, goals], axis=2), ((0, 0), (0, 0), (0, 110)))
-    peer = jnp.mod(partners - me + 8 + count, count)
-    match = jnp.arange(16)[:, None] == peer[None, :]
-    req = jnp.sum(jnp.where(match[:, :, None, None], rows[None], 0.0), axis=1)
-    named = targets.reshape(-1)[:, None] == jnp.arange(384)[None, :]
-    named = named & (jnp.arange(384)[None, :] < 320)
-    angle = jnp.sum(jnp.where(named, rotation[0, 0, 0].reshape(-1)[:, None], 0.0), axis=0)
-    cs = jnp.stack([jnp.cos(angle), jnp.sin(angle)])
     block = (components, width_p, levels, width_t)
     vm = pltpu.VMEM
     tile = (levels, width_t)
@@ -351,7 +356,7 @@
     xo, ro = pl.pallas_call(
         lambda *refs: kernel(colats, lons, *refs),
         out_shape=[jax.ShapeDtypeStruct(block, F32)] * 2,
-        in_specs=[pl.BlockSpec(memory_space=pltpu.VMEM)] * 6,
+        in_specs=[pl.BlockSpec(memory_space=pltpu.SMEM)] * 2 + [pl.BlockSpec(memory_space=pltpu.VMEM)] * 7,
         out_specs=[pl.BlockSpec(memory_space=pltpu.VMEM)] * 2,
         scratch_shapes=[
             vm((2, components, width_p + 2) + tile, F32),
@@ -359,21 +364,24 @@
             vm((width_p + 1,) + tile, F32),
             vm(row_tiles, F32), vm(row_tiles, F32), vm(row_tiles, F32), vm(row_tiles, F32),
             vm(row_tiles, F32), vm(row_tiles, F32),
-            vm((width_p // 2, 384, 256), BF16), vm((width_p // 2, 384, 256), BF16),
+            vm((384, width_p * width_t), BF16), vm((384, width_p * width_t), BF16),
+            vm((64, width_p * width_t), BF16),
             vm((384, 384), BF16),
-            vm((16,) + tile, F32),
+            vm((128, 128), F32),
+            vm((16,) + tile, F32), vm((16,) + tile, F32),
             vm((3, 2, components) + tile, F32), vm((3, 2, components) + tile, F32),
             vm((3, 2) + tile, F32), vm((3, 2) + tile, F32),
             vm((2,) + tile, F32), vm((2,) + tile, F32), vm((2,) + tile, F32),
             vm((3, 16) + tile, F32), vm((3, 16) + tile, F32),
             pltpu.SemaphoreType.DMA((16,)), pltpu.SemaphoreType.DMA((16,)),
-            pltpu.SemaphoreType.DMA((60,)), pltpu.SemaphoreType.DMA((60,)),
+            pltpu.SemaphoreType.DMA((4,)), pltpu.SemaphoreType.DMA((4,)),
         ],
         compiler_params=pltpu.CompilerParams(
             collective_id=0, has_side_effects=True, vmem_limit_bytes=32 * 1024 * 1024),
         name="sweeps",
-    )(act, jnp.transpose(state[0], (0, 2, 1, 3)), jnp.transpose(rhs[0], (0, 2, 1, 3)),
-      jnp.transpose(viscosity[0], (1, 0, 2)), req, cs)
+    )(radial_bounds, partner_device[0, 0, 0], jnp.transpose(state[0], (0, 2, 1, 3)),
+      jnp.transpose(rhs[0], (0, 2, 1, 3)), jnp.transpose(viscosity[0], (1, 0, 2)),
+      ghost_source[0, 0, 0], ghost_target[0, 0, 0], interp_weights[0, 0, 0], rotation[0, 0, 0])
     back = lambda x: jnp.transpose(x, (0, 2, 1, 3))[None]
     return back(xo), back(ro)
 

time: 66.5 us -> 44.6 us (0.67)
  Pallas kernels: 57.1 us -> 38.5 us
  other arithmetic: 1.77 us -> 0 us
  local copies, waits for them, and re-layouts: 6.51 us -> 5.23 us
    pallas_call x1, Pallas kernels: 57.1 us -> 38.5 us  [per_device(): pl.pallas_call(lambda *refs: kernel(colats, lons, *refs), out_shape=[jax....]
    convert_element_type x3 -> x0, other arithmetic: 1.3 us -> none  [the longest x1 1.29 us: per_device(): ((level_ids >= radial_bounds[0, 0]) & (level_ids < radial_bounds[0, 1]))....]
    unnamed x22 -> x15, local copies, waits for them, and re-layouts: 4.67 us -> 3.4 us
    transpose x1, local copies, waits for them, and re-layouts: 0.61 us -> 1.82 us  [per_device(): jnp.transpose(rhs[0], (0, 2, 1, 3))]
where the time goes in v1:
time: 44.6 us; the launch traced here: 44.5 us
  Pallas kernels  38.5 us (86%)
  local copies, waits for them, and re-layouts  5.23 us (12%)
  between operations  0.72 us (2%)
    pallas_call x1, Pallas kernels, per_device(): pl.pallas_call(lambda *refs: kernel(colats, lons, *refs), out_shape=[jax....  38.5 us
    unnamed x15, local copies, waits for them, and re-layouts  3.4 us
    transpose x1, local copies, waits for them, and re-layouts, per_device(): jnp.transpose(rhs[0], (0, 2, 1, 3))  1.82 us

profile of v1, /device:TPU:0, one launch (start us, length us, event | category | flops | bytes accessed | tf_op | source)
XLA Modules:
  0.0 44.5 jit_solution(1714567890718861041)
XLA Ops:
  0.6 1.0 %copy.19 = f32[1,8,32,128]{3,1,2,0:T(8,128)S(1)} copy(f32[1,8,32,128]{3,2,1,0:T(8,128)} %param.11) | data formatting | bytes 262144 | tf_op args[2]
  1.6 0.0 copy-start
  1.6 0.0 copy-start.1
  1.6 0.0 copy-start.2
  1.7 0.0 copy-start.3
  1.7 1.8 %copy_bitcast_fusion = (f32[4,32,8,128]{3,2,1,0:T(8,128)S(1)}, f32[4,32,8,128]{3,2,1,0:T(8,128)S(1)}) fusion(f32[1,4,8,32,128]{4,3,2,1,0:T(8,128)} %param.10, f32[1,4,8,32,128]{4,3,2,1,0:T(8,128)} %param.9), kind=kLoop, calls=%fused_computation | loop fusion | bytes 2097152 | tf_op jit(solution)/shard_map/transpose | solution.py:383
  3.5 0.0 copy-start.4
  3.5 0.0 copy-start.5
  3.5 0.0 copy-done
  3.5 0.0 copy-done.1
  3.5 0.0 copy-done.2
  3.5 0.0 copy-done.3
  3.6 0.6 %copy-done.4 = s32[1,2]{1,0:T(1,128)S(1)} copy-done((s32[1,2]{1,0:T(1,128)S(1)}, s32[1,2]{1,0:T(1,128)}, u32[]{:S(2)}) %copy-start.4) | copy-done | bytes 32
  4.1 0.0 copy-done.5
  4.2 38.5 %sweeps.1 = (f32[4,32,8,128]{3,2,1,0:T(8,128)S(1)}, f32[4,32,8,128]{3,2,1,0:T(8,128)S(1)}) custom-call(s32[1,2]{1,0:T(1,128)S(1)} %copy-done.4, s32[8]{0:T(128)S(1)} %bitcast.31, f32[4,32,8,128]{3,2,1,0:T(8,128)S(1)} %get-tuple-element.9.refs_2_, f32[4,32,8,128]{3,2,1,0:T(8,128)S(1)} %get-tuple-element.8.refs_3_, f32[32,8,128]{2,1,0:T(8,128)S(1)} %bitcast.26, ...), custom_call_target="tpu_custom_call" | custom-call | tf_op jit(solution)/shard_map/sweeps/pallas_call | solution.py:356
  42.7 0.9 %copy.14 = f32[1,4,8,32,128]{4,3,2,1,0:T(8,128)} copy(f32[1,4,8,32,128]{4,2,3,1,0:T(8,128)S(1)} %bitcast.25) | data formatting | bytes 1048576
  43.6 0.9 %copy.15 = f32[1,4,8,32,128]{4,3,2,1,0:T(8,128)} copy(f32[1,4,8,32,128]{4,2,3,1,0:T(8,128)S(1)} %bitcast.24) | data formatting | bytes 1048576
Async XLA Ops:
  1.6 1.9 %copy-start = (f32[1,1,1,8,4,20]{5,4,3,2,1,0:T(4,128)S(1)}, f32[1,1,1,8,4,20]{5,4,3,2,1,0:T(4,128)}, u32[]{:S(2)}) copy-start(f32[1,1,1,8,4,20]{5,4,3,2,1,0:T(4,128)} %param.16) | copy-start | bytes 7684
  1.6 1.9 %copy-start.1 = (s32[1,1,1,8,20]{4,3,2,1,0:T(8,128)S(1)}, s32[1,1,1,8,20]{4,3,2,1,0:T(8,128)}, u32[]{:S(2)}) copy-start(s32[1,1,1,8,20]{4,3,2,1,0:T(8,128)} %param.14) | copy-start | bytes 1924
  1.6 1.9 %copy-start.2 = (s32[1,1,1,8,20]{4,3,2,1,0:T(8,128)S(1)}, s32[1,1,1,8,20]{4,3,2,1,0:T(8,128)}, u32[]{:S(2)}) copy-start(s32[1,1,1,8,20]{4,3,2,1,0:T(8,128)} %param.15) | copy-start | bytes 1924
  1.7 1.9 %copy-start.3 = (f32[1,1,1,8,20]{4,3,2,1,0:T(8,128)S(1)}, f32[1,1,1,8,20]{4,3,2,1,0:T(8,128)}, u32[]{:S(2)}) copy-start(f32[1,1,1,8,20]{4,3,2,1,0:T(8,128)} %param.17) | copy-start | bytes 1924
  3.5 0.7 %copy-start.4 = (s32[1,2]{1,0:T(1,128)S(1)}, s32[1,2]{1,0:T(1,128)}, u32[]{:S(2)}) copy-start(s32[1,2]{1,0:T(1,128)} %refs_0_.1) | copy-start | bytes 28
  3.5 0.7 %copy-start.5 = (s32[1,1,1,8]{3,2,1,0:T(1,128)S(1)}, s32[1,1,1,8]{3,2,1,0:T(1,128)}, u32[]{:S(2)}) copy-start(s32[1,1,1,8]{3,2,1,0:T(1,128)} %param.13) | copy-start | bytes 100

commit v2 on v1

--- a/solution.py
+++ b/solution.py
@@ -22,11 +22,11 @@
     return lax.fori_loop(0, steps // unroll, block, init)
 
 
-def kernel(colats, lons, bounds_ref, partner_ref, state_ref, rhs_ref, visc_ref, src_ref, tgt_ref, w_ref, rot_ref,
+def kernel(colats, lons, bounds_ref, partner_ref, rhs_in, state_ref, visc_ref, src_ref, tgt_ref, w_ref, rot_ref,
            xo_ref, ro_ref,
-           mk, ve, klon, kcu, kcd, kru, krd, dg, dinv, whi, wlo, mhl, oh, fx, req_ref, rx,
+           rhs_ref, mk, ve, klon, kcu, kcd, kru, krd, dg, dinv, whi, wlo, mhl, oh, fx, req_ref, rx,
            slon, rlon, scol, rcol, vscol, vrcol, vrlon, sg, rg,
-           hsend, hrecv, gsend, grecv):
+           hsend, hrecv, gsend, grecv, loads):
     width = state_ref.shape[1]
     count = colats * lons
     panel = lax.axis_index("panel")
@@ -42,6 +42,12 @@
     lon_up = (panel, colat, lax.rem(lon + 1, lons))
     col_dn = (panel, lax.rem(colat + colats - 1, colats), lon)
     col_up = (panel, lax.rem(colat + 1, colats), lon)
+
+    rhs_loads = []
+    for l in range(8):
+        rhs_loads.append(pltpu.make_async_copy(rhs_in.at[:, l], rhs_ref.at[:, :, l], loads.at[l]))
+    for copy in rhs_loads:
+        copy.start()
 
     barrier = pltpu.get_barrier_semaphore()
     greeted = [o for o in range(-8, 9)][: min(17, count)]
@@ -263,6 +269,8 @@
 
     blocked(width, 4, links, 0)
 
+    for copy in rhs_loads:
+        copy.wait()
     for r in range(3):
         now, later = r % 2, (r + 1) % 2
         if r > 0:
@@ -356,9 +364,10 @@
     xo, ro = pl.pallas_call(
         lambda *refs: kernel(colats, lons, *refs),
         out_shape=[jax.ShapeDtypeStruct(block, F32)] * 2,
-        in_specs=[pl.BlockSpec(memory_space=pltpu.SMEM)] * 2 + [pl.BlockSpec(memory_space=pltpu.VMEM)] * 7,
+        in_specs=[pl.BlockSpec(memory_space=pltpu.SMEM)] * 2 + [pl.BlockSpec(memory_space=pl.ANY)] + [pl.BlockSpec(memory_space=pltpu.VMEM)] * 6,
         out_specs=[pl.BlockSpec(memory_space=pltpu.VMEM)] * 2,
         scratch_shapes=[
+            vm(block, F32),
             vm((2, components, width_p + 2) + tile, F32),
             vm((width_p + 2,) + tile, F32),
             vm((width_p + 1,) + tile, F32),
@@ -375,12 +384,13 @@
             vm((3, 16) + tile, F32), vm((3, 16) + tile, F32),
             pltpu.SemaphoreType.DMA((16,)), pltpu.SemaphoreType.DMA((16,)),
             pltpu.SemaphoreType.DMA((4,)), pltpu.SemaphoreType.DMA((4,)),
+            pltpu.SemaphoreType.DMA((8,)),
         ],
         compiler_params=pltpu.CompilerParams(
             collective_id=0, has_side_effects=True, vmem_limit_bytes=32 * 1024 * 1024),
         name="sweeps",
-    )(radial_bounds, partner_device[0, 0, 0], jnp.transpose(state[0], (0, 2, 1, 3)),
-      jnp.transpose(rhs[0], (0, 2, 1, 3)), jnp.transpose(viscosity[0], (1, 0, 2)),
+    )(radial_bounds, partner_device[0, 0, 0], rhs[0],
+      jnp.transpose(state[0], (0, 2, 1, 3)), jnp.transpose(viscosity[0], (1, 0, 2)),
       ghost_source[0, 0, 0], ghost_target[0, 0, 0], interp_weights[0, 0, 0], rotation[0, 0, 0])
     back = lambda x: jnp.transpose(x, (0, 2, 1, 3))[None]
     return back(xo), back(ro)

time: 44.6 us -> 44.7 us (level)
  Pallas kernels: 38.5 us -> 39 us
    transpose x1 -> x0, local copies, waits for them, and re-layouts: 1.82 us -> none  [per_device(): jnp.transpose(rhs[0], (0, 2, 1, 3))]
    unnamed x15 -> x18, local copies, waits for them, and re-layouts: 3.4 us -> 4.8 us
where the time goes in v2:
time: 44.7 us; the launch traced here: 44.5 us
  Pallas kernels  39 us (87%)
  local copies, waits for them, and re-layouts  4.8 us (11%)
  between operations  0.74 us (2%)
    pallas_call x1, Pallas kernels, per_device(): pl.pallas_call(lambda *refs: kernel(colats, lons, *refs), out_shape=[jax....  39 us
    unnamed x18, local copies, waits for them, and re-layouts  4.8 us

profile of v2, /device:TPU:0, one launch (start us, length us, event | category | flops | bytes accessed | tf_op | source)
XLA Modules:
  0.0 44.5 jit_solution(8837269976911801689)
XLA Ops:
  0.6 1.0 %copy.18 = f32[1,8,32,128]{3,1,2,0:T(8,128)S(1)} copy(f32[1,8,32,128]{3,2,1,0:T(8,128)} %param.11) | data formatting | bytes 262144 | tf_op args[2]
  1.6 0.0 copy-start
  1.6 0.0 copy-start.1
  1.6 0.0 copy-start.2
  1.7 0.0 copy-start.3
  1.7 0.0 copy-start.4
  1.7 1.4 %copy.17 = f32[1,4,8,32,128]{4,2,3,1,0:T(8,128)S(1)} copy(f32[1,4,8,32,128]{4,3,2,1,0:T(8,128)} %param.9) | data formatting | bytes 1048576 | tf_op args[0]
  3.1 0.0 copy-start.5
  3.1 0.0 copy-start.6
  3.1 0.0 copy-done
  3.1 0.0 copy-done.1
  3.1 0.0 copy-done.2
  3.1 0.0 copy-done.3
  3.1 0.0 copy-done.4
  3.2 0.6 %copy-done.5 = s32[1,2]{1,0:T(1,128)S(1)} copy-done((s32[1,2]{1,0:T(1,128)S(1)}, s32[1,2]{1,0:T(1,128)}, u32[]{:S(2)}) %copy-start.5) | copy-done | bytes 32
  3.7 0.0 copy-done.6
  3.8 39.0 %sweeps.1 = (f32[4,32,8,128]{3,2,1,0:T(8,128)S(1)}, f32[4,32,8,128]{3,2,1,0:T(8,128)S(1)}) custom-call(s32[1,2]{1,0:T(1,128)S(1)} %copy-done.5, s32[8]{0:T(128)S(1)} %bitcast.31, f32[4,8,32,128]{3,2,1,0:T(8,128)S(1)} %bitcast.23, f32[4,32,8,128]{3,2,1,0:T(8,128)S(1)} %bitcast.22, f32[32,8,128]{2,1,0:T(8,128)S(1)} %bitcast.26, s32[8,20]{1,0:T(8,128)S(1)} %bitcast.28, ...), custom_call_target="tpu_custom_call" | custom-call | tf_op jit(solution)/shard_map/sweeps/pallas_call | solution.py:364
  42.7 0.9 %copy.13 = f32[1,4,8,32,128]{4,3,2,1,0:T(8,128)} copy(f32[1,4,8,32,128]{4,2,3,1,0:T(8,128)S(1)} %bitcast.25) | data formatting | bytes 1048576
  43.6 0.9 %copy.14 = f32[1,4,8,32,128]{4,3,2,1,0:T(8,128)} copy(f32[1,4,8,32,128]{4,2,3,1,0:T(8,128)S(1)} %bitcast.24) | data formatting | bytes 1048576
Async XLA Ops:
  1.6 1.5 %copy-start = (f32[1,4,8,32,128]{4,3,2,1,0:T(8,128)S(1)}, f32[1,4,8,32,128]{4,3,2,1,0:T(8,128)}, u32[]{:S(2)}) copy-start(f32[1,4,8,32,128]{4,3,2,1,0:T(8,128)} %param.10) | copy-start | bytes 1572868
  1.6 1.5 %copy-start.1 = (f32[1,1,1,8,4,20]{5,4,3,2,1,0:T(4,128)S(1)}, f32[1,1,1,8,4,20]{5,4,3,2,1,0:T(4,128)}, u32[]{:S(2)}) copy-start(f32[1,1,1,8,4,20]{5,4,3,2,1,0:T(4,128)} %param.16) | copy-start | bytes 7684
  1.6 1.5 %copy-start.2 = (s32[1,1,1,8,20]{4,3,2,1,0:T(8,128)S(1)}, s32[1,1,1,8,20]{4,3,2,1,0:T(8,128)}, u32[]{:S(2)}) copy-start(s32[1,1,1,8,20]{4,3,2,1,0:T(8,128)} %param.14) | copy-start | bytes 1924
  1.7 1.5 %copy-start.3 = (s32[1,1,1,8,20]{4,3,2,1,0:T(8,128)S(1)}, s32[1,1,1,8,20]{4,3,2,1,0:T(8,128)}, u32[]{:S(2)}) copy-start(s32[1,1,1,8,20]{4,3,2,1,0:T(8,128)} %param.15) | copy-start | bytes 1924
  1.7 1.5 %copy-start.4 = (f32[1,1,1,8,20]{4,3,2,1,0:T(8,128)S(1)}, f32[1,1,1,8,20]{4,3,2,1,0:T(8,128)}, u32[]{:S(2)}) copy-start(f32[1,1,1,8,20]{4,3,2,1,0:T(8,128)} %param.17) | copy-start | bytes 1924
  3.1 0.7 %copy-start.5 = (s32[1,2]{1,0:T(1,128)S(1)}, s32[1,2]{1,0:T(1,128)}, u32[]{:S(2)}) copy-start(s32[1,2]{1,0:T(1,128)} %refs_0_.1) | copy-start | bytes 28
  3.1 0.7 %copy-start.6 = (s32[1,1,1,8]{3,2,1,0:T(1,128)S(1)}, s32[1,1,1,8]{3,2,1,0:T(1,128)}, u32[]{:S(2)}) copy-start(s32[1,1,1,8]{3,2,1,0:T(1,128)} %param.13) | copy-start | bytes 100
